TPU v7x, 512 devices: a whole 4x8x8 slice. The times are simulated.
512 devices in a mesh: txt: 16 (over y_hi, z), aud: 32 (over x, y_lo, core).
Axes of the slice: x: 4, y: 8 (y_hi: 2, y_lo: 4; y = y_hi * 4 + y_lo), z: 8, core: 2. Of those that a mesh axis runs over, the one named last changes fastest.
Arguments:
- images: float32 [131072, 1024], P(('txt', 'aud')), may hold values from -2 to 2
- texts: float32 [256, 1024], P('txt'), may hold values from -2 to 2
- audio: float32 [128, 1024], P('aud'), may hold values from -2 to 2
- pos_text: int32 [131072], P(('txt', 'aud')), may hold values from 0 to 255
- pos_audio: int32 [131072], P(('txt', 'aud')), may hold values from 0 to 11
- logit_scale: float32 [1], replicated, may hold values from 1 to 4
- logit_bias: float32 [1], replicated, may hold values from -3 to -1
Outputs:
- grad_images: float32 [131072, 1024], P(('txt', 'aud'))
- grad_texts: float32 [256, 1024], P('txt')
- grad_audio: float32 [128, 1024], P('aud')
All inputs are finite; a program needn't handle non-finite values.
Results may differ from a plain program's by a relative error of at most 0.0044.
Values sent between devices are 32-bit elements; how exact they have to be, the bound alone decides.
No kernel may reach another device: no remote copies, remote signals or barrier semaphores. Data moves between devices by JAX's collectives and lax.ppermute only.
A program may use at most 64 MiB of HBM per device.

v0:
```python
import jax
import jax.numpy as jnp
from jax import lax
from jax.sharding import PartitionSpec as P

HOPS = 2


def from_behind(shard, axis, by):
    size = lax.axis_size(axis)
    return lax.ppermute(shard, axis, [(i, (i + by) % size) for i in range(size)])


def block_terms(image_half, text_piece, window, first_row, pos_text, pos_audio, temper, offset):
    row_count = text_piece.shape[0]
    slot_count = window.shape[0]
    products = (
        (text_piece[:, None, :] * window[None, :, :])
        .reshape(row_count * slot_count, -1)
        .astype(jnp.bfloat16)
    )
    logits = (
        temper
        * lax.dot_general(
            image_half, products, (((1,), (1,)), ((), ())), preferred_element_type=jnp.float32
        )
        + offset
    )
    columns = jnp.arange(row_count * slot_count, dtype=jnp.int32)
    text_of = first_row + columns // slot_count
    slot_of = columns % slot_count
    positive = (text_of[None, :] == pos_text[:, None]) & (slot_of[None, :] == pos_audio[:, None])
    slope = ((jax.nn.sigmoid(logits) - positive.astype(jnp.float32)) * temper).astype(jnp.bfloat16)
    grad_image = jnp.dot(slope, products, preferred_element_type=jnp.float32)
    grad_prod = lax.dot_general(
        slope, image_half, (((0,), (0,)), ((), ())), preferred_element_type=jnp.float32
    )
    grad_prod = grad_prod.reshape(row_count, slot_count, -1)
    grad_piece = jnp.sum(grad_prod * window[None, :, :], axis=1)
    grad_window = jnp.sum(grad_prod * text_piece[:, None, :], axis=0)
    return (grad_image, grad_piece, grad_window)


def send_home(grad_window, block_rows):
    carried = grad_window[HOPS * block_rows :]
    for number in range(HOPS):
        level = HOPS - 1 - number
        carried = (
            from_behind(carried, "aud", 1)
            + grad_window[level * block_rows : (level + 1) * block_rows]
        )
    return carried


def shards(images, texts, audio, pos_text, pos_audio, logit_scale, logit_bias):
    temper = logit_scale[0]
    offset = logit_bias[0]
    block_rows = audio.shape[0]
    text_rows = texts.shape[0]
    pieces = [audio]
    current = audio
    for number in range(HOPS):
        current = from_behind(current, "aud", -1)
        pieces.append(current)
    window = jnp.concatenate(pieces, axis=0)
    image_half = images.astype(jnp.bfloat16)
    cycle_size = lax.axis_size("txt")
    position = lax.axis_index("txt")
    empty_image = jnp.zeros(images.shape, jnp.float32)
    empty_window = jnp.zeros(window.shape, jnp.float32)

    def advance(turn_index, state):
        held_text, held_grad, grad_image, grad_window = state
        owner = (position - turn_index) % cycle_size
        first = owner * text_rows
        more_image, more_piece, more_window = block_terms(
            image_half, held_text, window, first, pos_text, pos_audio, temper, offset
        )
        held_text, held_grad = from_behind((held_text, held_grad + more_piece), "txt", 1)
        return (held_text, held_grad, grad_image + more_image, grad_window + more_window)

    start_state = (texts, jnp.zeros(texts.shape, jnp.float32), empty_image, empty_window)
    final_state = lax.fori_loop(0, cycle_size, advance, start_state)
    grad_local_text = final_state[1]
    grad_images = final_state[2]
    grad_window = final_state[3]
    grad_texts = lax.psum(grad_local_text, "aud")
    summed_window = lax.psum(grad_window, "txt")
    grad_audio = send_home(summed_window, block_rows)
    return (grad_images, grad_texts, grad_audio)


def solution(mesh):
    placed = (
        P(("txt", "aud"), None),
        P("txt", None),
        P("aud", None),
        P(("txt", "aud")),
        P(("txt", "aud")),
        P(),
        P(),
    )
    return jax.shard_map(
        shards,
        mesh=mesh,
        in_specs=placed,
        out_specs=(P(("txt", "aud"), None), P("txt", None), P("aud", None)),
        check_vma=False,
    )
```

profile of v0, /device:TPU:32, one launch (start us, length us, event | category | flops | bytes accessed | tf_op | source)
XLA Modules:
  0.0 684.3 jit_solution(6114707449579966862)
XLA Ops:
  8.7 4.4 collective-permute-start.2
  14.6 7.5 %collective-permute-start.3 = (f32[4,1024]{1,0:T(4,128)S(1)}, f32[4,1024]{1,0:T(4,128)S(1)}, u32[]{:S(2)}, u32[]{:S(2)}) collective-permute-start(f32[4,1024]{1,0:T(4,128)S(1)} %collective-permute-done.2), channel_id=1, source_target_pairs={{0,31},{1,0},{2,1},{3,2},{4,3},{5,4},{6,5},{7,6},{8,7},{9,8},{10,9... | collective-permute-start | bytes 49160 | tf_op jit(solution)/shard_map/ppermute | solution.py:11
  24.2 301.3 %while.23 = (s32[]{:T(128)}, f32[16,1024]{1,0:T(8,128)}, f32[16,1024]{1,0:T(8,128)}, f32[256,1024]{1,0:T(8,128)S(1)}, f32[12,1024]{1,0:T(8,128)}, /*index=5*/f32...) while((s32[]{:T(128)}, f32[16,1024]{1,0:T(8,128)}, ...), condition=%wide.region_3.4_spmd.clone, body=%wide.region_0.3_spmd.clone.sunk | while | flops 304298432 | bytes 14095801 | solution.py:83
  25.1 4.3 collective-permute-start
  32.8 4.3 collective-permute-start.1
  59.8 4.6 collective-permute-done.1
  77.8 5.2 collective-permute-done.1
  96.2 5.3 collective-permute-done.1
  114.7 5.3 collective-permute-done.1
  133.2 5.4 collective-permute-done.1
  151.7 5.3 collective-permute-done.1
  170.2 5.6 collective-permute-done.1
  189.0 6.0 collective-permute-done.1
  208.9 4.7 collective-permute-done.1
  228.0 4.7 collective-permute-done.1
  242.7 4.4 collective-permute-done
  261.2 4.5 collective-permute-done
  283.9 4.5 collective-permute-done.1
  298.5 4.4 collective-permute-done
  320.7 4.9 collective-permute-done.1
  325.6 93.6 %psum.15 = f32[12,1024]{1,0:T(8,128)S(1)} all-reduce(f32[12,1024]{1,0:T(8,128)} %get-tuple-element.335), channel_id=1, replica_groups=mesh['txt'=16,'aud'=32] {'txt'}, use_global_device_ids=true, to_apply=%region_5.6 | all-reduce | flops 12288 | bytes 98304 | tf_op jit(solution)/shard_map/psum | solution.py:88
  421.1 7.0 %collective-permute-done.4 = f32[4,1024]{1,0:T(4,128)S(1)} collective-permute-done((f32[4,1024]{1,0:T(4,128)S(1)}, f32[4,1024]{1,0:T(4,128)S(1)}, u32[]{:S(2)}, u32[]{:S(2)}) %collective-permute-start.4) | collective-permute-done | bytes 16416 | tf_op jit(solution)/shard_map/ppermute | solution.py:11
  430.1 7.0 %collective-permute-done.5 = f32[4,1024]{1,0:T(4,128)S(1)} collective-permute-done((f32[4,1024]{1,0:T(4,128)S(1)}, f32[4,1024]{1,0:T(4,128)S(1)}, u32[]{:S(2)}, u32[]{:S(2)}) %collective-permute-start.5) | collective-permute-done | bytes 16416 | tf_op jit(solution)/shard_map/ppermute | solution.py:11
  437.8 238.2 %all-reduce.2.cloned.1.call-done = f32[16,1024]{1,0:T(8,128)} async-done(((f32[16,1024]{1,0:T(8,128)}), f32[16,1024]{1,0:T(8,128)}) %all-reduce.2.cloned.1.call-update) | async-done | bytes 65552 | tf_op jit(solution)/shard_map/psum | solution.py:87
  (311 shorter events, 226.8 us)
Async XLA Ops:
  7.2 668.8 %all-reduce.2.cloned.1.call-start = ((), (), s32[]{:S(2)}) async-start(), calls=%async_computation | async-start | bytes 131072 | tf_op jit(solution)/shard_map/psum | solution.py:87
  25.1 17.1 %collective-permute-start = (f32[16,1024]{1,0:T(8,128)S(1)}, f32[16,1024]{1,0:T(8,128)}, u32[]{:S(2)}, u32[]{:S(2)}) collective-permute-start(f32[16,1024]{1,0:T(8,128)S(1)} %copy.16), channel_id=1, source_target_pairs={{0,32},{32,64},{64,96},{96,128},{128,160},{160,192},{192,224},{224... | collective-permute-start | bytes 196616 | tf_op jit(solution)/shard_map/while/body/eval_jaxpr/ppermute | solution.py:11
  32.8 13.2 %collective-permute-start.1 = (f32[16,1024]{1,0:T(8,128)S(1)}, f32[16,1024]{1,0:T(8,128)}, u32[]{:S(2)}, u32[]{:S(2)}) collective-permute-start(f32[16,1024]{1,0:T(8,128)S(1)} %add.228), channel_id=1, source_target_pairs={{0,32},{32,64},{64,96},{96,128},{128,160},{160,192},{192,224},{224... | collective-permute-start | bytes 196616 | tf_op jit(solution)/shard_map/while/body/eval_jaxpr/ppermute | solution.py:11
  46.9 13.0 %collective-permute-start = (f32[16,1024]{1,0:T(8,128)S(1)}, f32[16,1024]{1,0:T(8,128)}, u32[]{:S(2)}, u32[]{:S(2)}) collective-permute-start(f32[16,1024]{1,0:T(8,128)S(1)} %copy.16), channel_id=1, source_target_pairs={{0,32},{32,64},{64,96},{96,128},{128,160},{160,192},{192,224},{224... | collective-permute-start | bytes 196616 | tf_op jit(solution)/shard_map/while/body/eval_jaxpr/ppermute | solution.py:11
  52.2 12.3 %collective-permute-start.1 = (f32[16,1024]{1,0:T(8,128)S(1)}, f32[16,1024]{1,0:T(8,128)}, u32[]{:S(2)}, u32[]{:S(2)}) collective-permute-start(f32[16,1024]{1,0:T(8,128)S(1)} %add.228), channel_id=1, source_target_pairs={{0,32},{32,64},{64,96},{96,128},{128,160},{160,192},{192,224},{224... | collective-permute-start | bytes 196616 | tf_op jit(solution)/shard_map/while/body/eval_jaxpr/ppermute | solution.py:11
  65.4 12.4 %collective-permute-start = (f32[16,1024]{1,0:T(8,128)S(1)}, f32[16,1024]{1,0:T(8,128)}, u32[]{:S(2)}, u32[]{:S(2)}) collective-permute-start(f32[16,1024]{1,0:T(8,128)S(1)} %copy.16), channel_id=1, source_target_pairs={{0,32},{32,64},{64,96},{96,128},{128,160},{160,192},{192,224},{224... | collective-permute-start | bytes 196616 | tf_op jit(solution)/shard_map/while/body/eval_jaxpr/ppermute | solution.py:11
  70.7 12.3 %collective-permute-start.1 = (f32[16,1024]{1,0:T(8,128)S(1)}, f32[16,1024]{1,0:T(8,128)}, u32[]{:S(2)}, u32[]{:S(2)}) collective-permute-start(f32[16,1024]{1,0:T(8,128)S(1)} %add.228), channel_id=1, source_target_pairs={{0,32},{32,64},{64,96},{96,128},{128,160},{160,192},{192,224},{224... | collective-permute-start | bytes 196616 | tf_op jit(solution)/shard_map/while/body/eval_jaxpr/ppermute | solution.py:11
  89.2 12.3 %collective-permute-start.1 = (f32[16,1024]{1,0:T(8,128)S(1)}, f32[16,1024]{1,0:T(8,128)}, u32[]{:S(2)}, u32[]{:S(2)}) collective-permute-start(f32[16,1024]{1,0:T(8,128)S(1)} %add.228), channel_id=1, source_target_pairs={{0,32},{32,64},{64,96},{96,128},{128,160},{160,192},{192,224},{224... | collective-permute-start | bytes 196616 | tf_op jit(solution)/shard_map/while/body/eval_jaxpr/ppermute | solution.py:11
  107.7 12.3 %collective-permute-start.1 = (f32[16,1024]{1,0:T(8,128)S(1)}, f32[16,1024]{1,0:T(8,128)}, u32[]{:S(2)}, u32[]{:S(2)}) collective-permute-start(f32[16,1024]{1,0:T(8,128)S(1)} %add.228), channel_id=1, source_target_pairs={{0,32},{32,64},{64,96},{96,128},{128,160},{160,192},{192,224},{224... | collective-permute-start | bytes 196616 | tf_op jit(solution)/shard_map/while/body/eval_jaxpr/ppermute | solution.py:11
  126.2 12.3 %collective-permute-start.1 = (f32[16,1024]{1,0:T(8,128)S(1)}, f32[16,1024]{1,0:T(8,128)}, u32[]{:S(2)}, u32[]{:S(2)}) collective-permute-start(f32[16,1024]{1,0:T(8,128)S(1)} %add.228), channel_id=1, source_target_pairs={{0,32},{32,64},{64,96},{96,128},{128,160},{160,192},{192,224},{224... | collective-permute-start | bytes 196616 | tf_op jit(solution)/shard_map/while/body/eval_jaxpr/ppermute | solution.py:11
  163.3 12.6 %collective-permute-start.1 = (f32[16,1024]{1,0:T(8,128)S(1)}, f32[16,1024]{1,0:T(8,128)}, u32[]{:S(2)}, u32[]{:S(2)}) collective-permute-start(f32[16,1024]{1,0:T(8,128)S(1)} %add.228), channel_id=1, source_target_pairs={{0,32},{32,64},{64,96},{96,128},{128,160},{160,192},{192,224},{224... | collective-permute-start | bytes 196616 | tf_op jit(solution)/shard_map/while/body/eval_jaxpr/ppermute | solution.py:11
  182.1 13.0 %collective-permute-start.1 = (f32[16,1024]{1,0:T(8,128)S(1)}, f32[16,1024]{1,0:T(8,128)}, u32[]{:S(2)}, u32[]{:S(2)}) collective-permute-start(f32[16,1024]{1,0:T(8,128)S(1)} %add.228), channel_id=1, source_target_pairs={{0,32},{32,64},{64,96},{96,128},{128,160},{160,192},{192,224},{224... | collective-permute-start | bytes 196616 | tf_op jit(solution)/shard_map/while/body/eval_jaxpr/ppermute | solution.py:11
  196.0 13.0 %collective-permute-start = (f32[16,1024]{1,0:T(8,128)S(1)}, f32[16,1024]{1,0:T(8,128)}, u32[]{:S(2)}, u32[]{:S(2)}) collective-permute-start(f32[16,1024]{1,0:T(8,128)S(1)} %copy.16), channel_id=1, source_target_pairs={{0,32},{32,64},{64,96},{96,128},{128,160},{160,192},{192,224},{224... | collective-permute-start | bytes 196616 | tf_op jit(solution)/shard_map/while/body/eval_jaxpr/ppermute | solution.py:11
  201.3 12.4 %collective-permute-start.1 = (f32[16,1024]{1,0:T(8,128)S(1)}, f32[16,1024]{1,0:T(8,128)}, u32[]{:S(2)}, u32[]{:S(2)}) collective-permute-start(f32[16,1024]{1,0:T(8,128)S(1)} %add.228), channel_id=1, source_target_pairs={{0,32},{32,64},{64,96},{96,128},{128,160},{160,192},{192,224},{224... | collective-permute-start | bytes 196616 | tf_op jit(solution)/shard_map/while/body/eval_jaxpr/ppermute | solution.py:11
  214.6 13.4 %collective-permute-start = (f32[16,1024]{1,0:T(8,128)S(1)}, f32[16,1024]{1,0:T(8,128)}, u32[]{:S(2)}, u32[]{:S(2)}) collective-permute-start(f32[16,1024]{1,0:T(8,128)S(1)} %copy.16), channel_id=1, source_target_pairs={{0,32},{32,64},{64,96},{96,128},{128,160},{160,192},{192,224},{224... | collective-permute-start | bytes 196616 | tf_op jit(solution)/shard_map/while/body/eval_jaxpr/ppermute | solution.py:11
  219.9 12.7 %collective-permute-start.1 = (f32[16,1024]{1,0:T(8,128)S(1)}, f32[16,1024]{1,0:T(8,128)}, u32[]{:S(2)}, u32[]{:S(2)}) collective-permute-start(f32[16,1024]{1,0:T(8,128)S(1)} %add.228), channel_id=1, source_target_pairs={{0,32},{32,64},{64,96},{96,128},{128,160},{160,192},{192,224},{224... | collective-permute-start | bytes 196616 | tf_op jit(solution)/shard_map/while/body/eval_jaxpr/ppermute | solution.py:11
  233.5 13.5 %collective-permute-start = (f32[16,1024]{1,0:T(8,128)S(1)}, f32[16,1024]{1,0:T(8,128)}, u32[]{:S(2)}, u32[]{:S(2)}) collective-permute-start(f32[16,1024]{1,0:T(8,128)S(1)} %copy.16), channel_id=1, source_target_pairs={{0,32},{32,64},{64,96},{96,128},{128,160},{160,192},{192,224},{224... | collective-permute-start | bytes 196616 | tf_op jit(solution)/shard_map/while/body/eval_jaxpr/ppermute | solution.py:11
  252.1 13.7 %collective-permute-start = (f32[16,1024]{1,0:T(8,128)S(1)}, f32[16,1024]{1,0:T(8,128)}, u32[]{:S(2)}, u32[]{:S(2)}) collective-permute-start(f32[16,1024]{1,0:T(8,128)S(1)} %copy.16), channel_id=1, source_target_pairs={{0,32},{32,64},{64,96},{96,128},{128,160},{160,192},{192,224},{224... | collective-permute-start | bytes 196616 | tf_op jit(solution)/shard_map/while/body/eval_jaxpr/ppermute | solution.py:11
  270.6 13.4 %collective-permute-start = (f32[16,1024]{1,0:T(8,128)S(1)}, f32[16,1024]{1,0:T(8,128)}, u32[]{:S(2)}, u32[]{:S(2)}) collective-permute-start(f32[16,1024]{1,0:T(8,128)S(1)} %copy.16), channel_id=1, source_target_pairs={{0,32},{32,64},{64,96},{96,128},{128,160},{160,192},{192,224},{224... | collective-permute-start | bytes 196616 | tf_op jit(solution)/shard_map/while/body/eval_jaxpr/ppermute | solution.py:11
  275.9 12.6 %collective-permute-start.1 = (f32[16,1024]{1,0:T(8,128)S(1)}, f32[16,1024]{1,0:T(8,128)}, u32[]{:S(2)}, u32[]{:S(2)}) collective-permute-start(f32[16,1024]{1,0:T(8,128)S(1)} %add.228), channel_id=1, source_target_pairs={{0,32},{32,64},{64,96},{96,128},{128,160},{160,192},{192,224},{224... | collective-permute-start | bytes 196616 | tf_op jit(solution)/shard_map/while/body/eval_jaxpr/ppermute | solution.py:11
  289.4 13.6 %collective-permute-start = (f32[16,1024]{1,0:T(8,128)S(1)}, f32[16,1024]{1,0:T(8,128)}, u32[]{:S(2)}, u32[]{:S(2)}) collective-permute-start(f32[16,1024]{1,0:T(8,128)S(1)} %copy.16), channel_id=1, source_target_pairs={{0,32},{32,64},{64,96},{96,128},{128,160},{160,192},{192,224},{224... | collective-permute-start | bytes 196616 | tf_op jit(solution)/shard_map/while/body/eval_jaxpr/ppermute | solution.py:11
  294.7 12.3 %collective-permute-start.1 = (f32[16,1024]{1,0:T(8,128)S(1)}, f32[16,1024]{1,0:T(8,128)}, u32[]{:S(2)}, u32[]{:S(2)}) collective-permute-start(f32[16,1024]{1,0:T(8,128)S(1)} %add.228), channel_id=1, source_target_pairs={{0,32},{32,64},{64,96},{96,128},{128,160},{160,192},{192,224},{224... | collective-permute-start | bytes 196616 | tf_op jit(solution)/shard_map/while/body/eval_jaxpr/ppermute | solution.py:11
  307.9 12.8 %collective-permute-start = (f32[16,1024]{1,0:T(8,128)S(1)}, f32[16,1024]{1,0:T(8,128)}, u32[]{:S(2)}, u32[]{:S(2)}) collective-permute-start(f32[16,1024]{1,0:T(8,128)S(1)} %copy.16), channel_id=1, source_target_pairs={{0,32},{32,64},{64,96},{96,128},{128,160},{160,192},{192,224},{224... | collective-permute-start | bytes 196616 | tf_op jit(solution)/shard_map/while/body/eval_jaxpr/ppermute | solution.py:11
  313.2 12.4 %collective-permute-start.1 = (f32[16,1024]{1,0:T(8,128)S(1)}, f32[16,1024]{1,0:T(8,128)}, u32[]{:S(2)}, u32[]{:S(2)}) collective-permute-start(f32[16,1024]{1,0:T(8,128)S(1)} %add.228), channel_id=1, source_target_pairs={{0,32},{32,64},{64,96},{96,128},{128,160},{160,192},{192,224},{224... | collective-permute-start | bytes 196616 | tf_op jit(solution)/shard_map/while/body/eval_jaxpr/ppermute | solution.py:11
  (49 other events, 741.6 us)
Sparse Core Ops, SparseCore 0:
  430.3 245.6 all-reduce.1
where the time goes:
time: 688 us; the launch traced here: 684 us
  waiting for transfers between devices  390 us (57%)
  blocking collectives  93.6 us (14%)
  starting transfers between devices  81.8 us (12%)
  other arithmetic  44.6 us (6%)
  matrix products  37.1 us (5%)
  local copies, waits for them, and re-layouts  20.8 us (3%)
  between operations  14.1 us (2%)
    psum x1, waiting for transfers between devices, shards(): grad_texts = lax.psum(grad_local_text, 'aud')  238 us
    ppermute x36, waiting for transfers between devices, from_behind(): lax.ppermute(shard, axis, [(i, (i + by) % size) for i in range(size)])  152 us
    psum x1, blocking collectives, shards(): summed_window = lax.psum(grad_window, 'txt')  93.6 us
    ppermute x36, starting transfers between devices, from_behind(): lax.ppermute(shard, axis, [(i, (i + by) % size) for i in range(size)])  81.7 us
    dot_general x16, matrix products, block_terms(): lax.dot_general(image_half, products, (((1,), (1,)), ((), ())), preferred...  26.5 us
    add x16, other arithmetic, advance(): grad_window + more_window  23 us
    while x80, local copies, waits for them, and re-layouts  14.4 us
  transfers between devices with their start and end apart: 37, of which 37 were waited for; matrix products, arithmetic and copies ran while one was open for 12% of the time, Pallas kernels for 0%

commit v1 on v0

--- a/solution.py
+++ b/solution.py
@@ -84,7 +84,7 @@
     grad_local_text = final_state[1]
     grad_images = final_state[2]
     grad_window = final_state[3]
-    grad_texts = lax.psum(grad_local_text, "aud")
+    grad_texts = jnp.sum(lax.all_gather(grad_local_text, "aud"), axis=0)
     summed_window = lax.psum(grad_window, "txt")
     grad_audio = send_home(summed_window, block_rows)
     return (grad_images, grad_texts, grad_audio)

time: 688 us -> 465 us (0.68)
  waiting for transfers between devices: 390 us -> 153 us
  matrix products: 37.1 us -> 48.3 us
    psum x1 -> x0, waiting for transfers between devices: 238 us -> none  [shards(): grad_texts = lax.psum(grad_local_text, 'aud')]
    dot_general x16, matrix products: 26.5 us -> 37.7 us  [block_terms(): lax.dot_general(image_half, products, (((1,), (1,)), ((), ())), preferred...]
  transfers between devices with their start and end apart: 37 -> 37, of which waited for: 37 -> 36; matrix products, arithmetic and copies ran while one was open for 12% -> 21% of each run, Pallas kernels for 0% -> 0%
where the time goes in v1:
time: 465 us; the launch traced here: 461 us
  waiting for transfers between devices  153 us (33%)
  blocking collectives  94 us (20%)
  starting transfers between devices  81.8 us (18%)
  other arithmetic  48.6 us (10%)
  matrix products  48.3 us (10%)
  local copies, waits for them, and re-layouts  19.3 us (4%)
  between operations  14.1 us (3%)
    ppermute x36, waiting for transfers between devices, from_behind(): lax.ppermute(shard, axis, [(i, (i + by) % size) for i in range(size)])  153 us
    psum x1, blocking collectives, shards(): summed_window = lax.psum(grad_window, 'txt')  94 us
    ppermute x36, starting transfers between devices, from_behind(): lax.ppermute(shard, axis, [(i, (i + by) % size) for i in range(size)])  81.7 us
    dot_general x16, matrix products, block_terms(): lax.dot_general(image_half, products, (((1,), (1,)), ((), ())), preferred...  37.7 us
    add x16, other arithmetic, advance(): grad_window + more_window  23 us
    add x16, other arithmetic, advance(): held_grad + more_piece  14.5 us
    while x80, local copies, waits for them, and re-layouts  14.4 us
  transfers between devices with their start and end apart: 37, of which 36 were waited for; matrix products, arithmetic and copies ran while one was open for 21% of the time, Pallas kernels for 0%

profile of v1, /device:TPU:32, one launch (start us, length us, event | category | flops | bytes accessed | tf_op | source)
XLA Modules:
  0.0 460.9 jit_solution(12938403948139987219)
XLA Ops:
  8.7 4.4 collective-permute-start.2
  14.7 7.5 %collective-permute-start.3 = (f32[4,1024]{1,0:T(4,128)S(1)}, f32[4,1024]{1,0:T(4,128)S(1)}, u32[]{:S(2)}, u32[]{:S(2)}) collective-permute-start(f32[4,1024]{1,0:T(4,128)S(1)} %collective-permute-done.2), channel_id=1, source_target_pairs={{0,31},{1,0},{2,1},{3,2},{4,3},{5,4},{6,5},{7,6},{8,7},{9,8},{10,9... | collective-permute-start | bytes 49160 | tf_op jit(solution)/shard_map/ppermute | solution.py:11
  25.1 314.1 %while.23 = (s32[]{:T(128)}, f32[16,1024]{1,0:T(8,128)}, f32[16,1024]{1,0:T(8,128)}, f32[256,1024]{1,0:T(8,128)S(1)}, f32[12,1024]{1,0:T(8,128)}, /*index=5*/f32...) while((s32[]{:T(128)}, f32[16,1024]{1,0:T(8,128)}, ...), condition=%wide.region_3.4_spmd.clone, body=%wide.region_0.3_spmd.clone.sunk | while | flops 304298432 | bytes 14095801 | solution.py:83
  25.9 4.3 collective-permute-start
  34.4 4.3 collective-permute-start.1
  42.0 5.6 %collective-permute-done.1 = f32[16,1024]{1,0:T(8,128)} collective-permute-done((f32[16,1024]{1,0:T(8,128)S(1)}, f32[16,1024]{1,0:T(8,128)}, u32[]{:S(2)}, u32[]{:S(2)}) %collective-permute-start.1) | collective-permute-done | bytes 65568 | tf_op jit(solution)/shard_map/while/body/eval_jaxpr/ppermute | solution.py:11
  61.1 5.8 %collective-permute-done.1 = f32[16,1024]{1,0:T(8,128)} collective-permute-done((f32[16,1024]{1,0:T(8,128)S(1)}, f32[16,1024]{1,0:T(8,128)}, u32[]{:S(2)}, u32[]{:S(2)}) %collective-permute-start.1) | collective-permute-done | bytes 65568 | tf_op jit(solution)/shard_map/while/body/eval_jaxpr/ppermute | solution.py:11
  80.7 5.4 %collective-permute-done.1 = f32[16,1024]{1,0:T(8,128)} collective-permute-done((f32[16,1024]{1,0:T(8,128)S(1)}, f32[16,1024]{1,0:T(8,128)}, u32[]{:S(2)}, u32[]{:S(2)}) %collective-permute-start.1) | collective-permute-done | bytes 65568 | tf_op jit(solution)/shard_map/while/body/eval_jaxpr/ppermute | solution.py:11
  99.3 6.1 %collective-permute-done.1 = f32[16,1024]{1,0:T(8,128)} collective-permute-done((f32[16,1024]{1,0:T(8,128)S(1)}, f32[16,1024]{1,0:T(8,128)}, u32[]{:S(2)}, u32[]{:S(2)}) %collective-permute-start.1) | collective-permute-done | bytes 65568 | tf_op jit(solution)/shard_map/while/body/eval_jaxpr/ppermute | solution.py:11
  118.5 6.2 %collective-permute-done.1 = f32[16,1024]{1,0:T(8,128)} collective-permute-done((f32[16,1024]{1,0:T(8,128)S(1)}, f32[16,1024]{1,0:T(8,128)}, u32[]{:S(2)}, u32[]{:S(2)}) %collective-permute-start.1) | collective-permute-done | bytes 65568 | tf_op jit(solution)/shard_map/while/body/eval_jaxpr/ppermute | solution.py:11
  137.9 6.2 %collective-permute-done.1 = f32[16,1024]{1,0:T(8,128)} collective-permute-done((f32[16,1024]{1,0:T(8,128)S(1)}, f32[16,1024]{1,0:T(8,128)}, u32[]{:S(2)}, u32[]{:S(2)}) %collective-permute-start.1) | collective-permute-done | bytes 65568 | tf_op jit(solution)/shard_map/while/body/eval_jaxpr/ppermute | solution.py:11
  157.2 6.4 %collective-permute-done.1 = f32[16,1024]{1,0:T(8,128)} collective-permute-done((f32[16,1024]{1,0:T(8,128)S(1)}, f32[16,1024]{1,0:T(8,128)}, u32[]{:S(2)}, u32[]{:S(2)}) %collective-permute-start.1) | collective-permute-done | bytes 65568 | tf_op jit(solution)/shard_map/while/body/eval_jaxpr/ppermute | solution.py:11
  176.8 6.1 %collective-permute-done.1 = f32[16,1024]{1,0:T(8,128)} collective-permute-done((f32[16,1024]{1,0:T(8,128)S(1)}, f32[16,1024]{1,0:T(8,128)}, u32[]{:S(2)}, u32[]{:S(2)}) %collective-permute-start.1) | collective-permute-done | bytes 65568 | tf_op jit(solution)/shard_map/while/body/eval_jaxpr/ppermute | solution.py:11
  196.0 6.8 %collective-permute-done.1 = f32[16,1024]{1,0:T(8,128)} collective-permute-done((f32[16,1024]{1,0:T(8,128)S(1)}, f32[16,1024]{1,0:T(8,128)}, u32[]{:S(2)}, u32[]{:S(2)}) %collective-permute-start.1) | collective-permute-done | bytes 65568 | tf_op jit(solution)/shard_map/while/body/eval_jaxpr/ppermute | solution.py:11
  216.0 6.1 %collective-permute-done.1 = f32[16,1024]{1,0:T(8,128)} collective-permute-done((f32[16,1024]{1,0:T(8,128)S(1)}, f32[16,1024]{1,0:T(8,128)}, u32[]{:S(2)}, u32[]{:S(2)}) %collective-permute-start.1) | collective-permute-done | bytes 65568 | tf_op jit(solution)/shard_map/while/body/eval_jaxpr/ppermute | solution.py:11
  235.4 6.1 %collective-permute-done.1 = f32[16,1024]{1,0:T(8,128)} collective-permute-done((f32[16,1024]{1,0:T(8,128)S(1)}, f32[16,1024]{1,0:T(8,128)}, u32[]{:S(2)}, u32[]{:S(2)}) %collective-permute-start.1) | collective-permute-done | bytes 65568 | tf_op jit(solution)/shard_map/while/body/eval_jaxpr/ppermute | solution.py:11
  255.4 6.1 %collective-permute-done.1 = f32[16,1024]{1,0:T(8,128)} collective-permute-done((f32[16,1024]{1,0:T(8,128)S(1)}, f32[16,1024]{1,0:T(8,128)}, u32[]{:S(2)}, u32[]{:S(2)}) %collective-permute-start.1) | collective-permute-done | bytes 65568 | tf_op jit(solution)/shard_map/while/body/eval_jaxpr/ppermute | solution.py:11
  274.7 6.1 %collective-permute-done.1 = f32[16,1024]{1,0:T(8,128)} collective-permute-done((f32[16,1024]{1,0:T(8,128)S(1)}, f32[16,1024]{1,0:T(8,128)}, u32[]{:S(2)}, u32[]{:S(2)}) %collective-permute-start.1) | collective-permute-done | bytes 65568 | tf_op jit(solution)/shard_map/while/body/eval_jaxpr/ppermute | solution.py:11
  294.4 6.1 %collective-permute-done.1 = f32[16,1024]{1,0:T(8,128)} collective-permute-done((f32[16,1024]{1,0:T(8,128)S(1)}, f32[16,1024]{1,0:T(8,128)}, u32[]{:S(2)}, u32[]{:S(2)}) %collective-permute-start.1) | collective-permute-done | bytes 65568 | tf_op jit(solution)/shard_map/while/body/eval_jaxpr/ppermute | solution.py:11
  313.7 6.1 %collective-permute-done.1 = f32[16,1024]{1,0:T(8,128)} collective-permute-done((f32[16,1024]{1,0:T(8,128)S(1)}, f32[16,1024]{1,0:T(8,128)}, u32[]{:S(2)}, u32[]{:S(2)}) %collective-permute-start.1) | collective-permute-done | bytes 65568 | tf_op jit(solution)/shard_map/while/body/eval_jaxpr/ppermute | solution.py:11
  333.0 6.2 %collective-permute-done.1 = f32[16,1024]{1,0:T(8,128)} collective-permute-done((f32[16,1024]{1,0:T(8,128)S(1)}, f32[16,1024]{1,0:T(8,128)}, u32[]{:S(2)}, u32[]{:S(2)}) %collective-permute-start.1) | collective-permute-done | bytes 65568 | tf_op jit(solution)/shard_map/while/body/eval_jaxpr/ppermute | solution.py:11
  339.2 94.0 %psum.7 = f32[12,1024]{1,0:T(8,128)S(1)} all-reduce(f32[12,1024]{1,0:T(8,128)} %get-tuple-element.335), channel_id=1, replica_groups=mesh['txt'=16,'aud'=32] {'txt'}, use_global_device_ids=true, to_apply=%region_5.6 | all-reduce | flops 12288 | bytes 98304 | tf_op jit(solution)/shard_map/psum | solution.py:88
  435.1 7.0 %collective-permute-done.4 = f32[4,1024]{1,0:T(4,128)S(1)} collective-permute-done((f32[4,1024]{1,0:T(4,128)S(1)}, f32[4,1024]{1,0:T(4,128)S(1)}, u32[]{:S(2)}, u32[]{:S(2)}) %collective-permute-start.4) | collective-permute-done | bytes 16416 | tf_op jit(solution)/shard_map/ppermute | solution.py:11
  444.1 7.0 %collective-permute-done.5 = f32[4,1024]{1,0:T(4,128)S(1)} collective-permute-done((f32[4,1024]{1,0:T(4,128)S(1)}, f32[4,1024]{1,0:T(4,128)S(1)}, u32[]{:S(2)}, u32[]{:S(2)}) %collective-permute-start.5) | collective-permute-done | bytes 16416 | tf_op jit(solution)/shard_map/ppermute | solution.py:11
  (305 shorter events, 219.1 us)
Async XLA Ops:
  7.2 444.6 %all-gather.3.cloned.1.call-start = ((), (), s32[]{:S(2)}) async-start(), calls=%async_computation | async-start | bytes 2162688 | tf_op jit(solution)/shard_map/all_gather | solution.py:87
  25.9 16.0 %collective-permute-start = (f32[16,1024]{1,0:T(8,128)S(1)}, f32[16,1024]{1,0:T(8,128)}, u32[]{:S(2)}, u32[]{:S(2)}) collective-permute-start(f32[16,1024]{1,0:T(8,128)S(1)} %copy.16), channel_id=1, source_target_pairs={{0,32},{32,64},{64,96},{96,128},{128,160},{160,192},{192,224},{224... | collective-permute-start | bytes 196616 | tf_op jit(solution)/shard_map/while/body/eval_jaxpr/ppermute | solution.py:11
  34.4 13.2 %collective-permute-start.1 = (f32[16,1024]{1,0:T(8,128)S(1)}, f32[16,1024]{1,0:T(8,128)}, u32[]{:S(2)}, u32[]{:S(2)}) collective-permute-start(f32[16,1024]{1,0:T(8,128)S(1)} %add.226), channel_id=1, source_target_pairs={{0,32},{32,64},{64,96},{96,128},{128,160},{160,192},{192,224},{224... | collective-permute-start | bytes 196616 | tf_op jit(solution)/shard_map/while/body/eval_jaxpr/ppermute | solution.py:11
  48.5 12.6 %collective-permute-start = (f32[16,1024]{1,0:T(8,128)S(1)}, f32[16,1024]{1,0:T(8,128)}, u32[]{:S(2)}, u32[]{:S(2)}) collective-permute-start(f32[16,1024]{1,0:T(8,128)S(1)} %copy.16), channel_id=1, source_target_pairs={{0,32},{32,64},{64,96},{96,128},{128,160},{160,192},{192,224},{224... | collective-permute-start | bytes 196616 | tf_op jit(solution)/shard_map/while/body/eval_jaxpr/ppermute | solution.py:11
  54.6 12.3 %collective-permute-start.1 = (f32[16,1024]{1,0:T(8,128)S(1)}, f32[16,1024]{1,0:T(8,128)}, u32[]{:S(2)}, u32[]{:S(2)}) collective-permute-start(f32[16,1024]{1,0:T(8,128)S(1)} %add.226), channel_id=1, source_target_pairs={{0,32},{32,64},{64,96},{96,128},{128,160},{160,192},{192,224},{224... | collective-permute-start | bytes 196616 | tf_op jit(solution)/shard_map/while/body/eval_jaxpr/ppermute | solution.py:11
  67.7 13.0 %collective-permute-start = (f32[16,1024]{1,0:T(8,128)S(1)}, f32[16,1024]{1,0:T(8,128)}, u32[]{:S(2)}, u32[]{:S(2)}) collective-permute-start(f32[16,1024]{1,0:T(8,128)S(1)} %copy.16), channel_id=1, source_target_pairs={{0,32},{32,64},{64,96},{96,128},{128,160},{160,192},{192,224},{224... | collective-permute-start | bytes 196616 | tf_op jit(solution)/shard_map/while/body/eval_jaxpr/ppermute | solution.py:11
  73.8 12.3 %collective-permute-start.1 = (f32[16,1024]{1,0:T(8,128)S(1)}, f32[16,1024]{1,0:T(8,128)}, u32[]{:S(2)}, u32[]{:S(2)}) collective-permute-start(f32[16,1024]{1,0:T(8,128)S(1)} %add.226), channel_id=1, source_target_pairs={{0,32},{32,64},{64,96},{96,128},{128,160},{160,192},{192,224},{224... | collective-permute-start | bytes 196616 | tf_op jit(solution)/shard_map/while/body/eval_jaxpr/ppermute | solution.py:11
  87.0 12.3 %collective-permute-start = (f32[16,1024]{1,0:T(8,128)S(1)}, f32[16,1024]{1,0:T(8,128)}, u32[]{:S(2)}, u32[]{:S(2)}) collective-permute-start(f32[16,1024]{1,0:T(8,128)S(1)} %copy.16), channel_id=1, source_target_pairs={{0,32},{32,64},{64,96},{96,128},{128,160},{160,192},{192,224},{224... | collective-permute-start | bytes 196616 | tf_op jit(solution)/shard_map/while/body/eval_jaxpr/ppermute | solution.py:11
  93.1 12.3 %collective-permute-start.1 = (f32[16,1024]{1,0:T(8,128)S(1)}, f32[16,1024]{1,0:T(8,128)}, u32[]{:S(2)}, u32[]{:S(2)}) collective-permute-start(f32[16,1024]{1,0:T(8,128)S(1)} %add.226), channel_id=1, source_target_pairs={{0,32},{32,64},{64,96},{96,128},{128,160},{160,192},{192,224},{224... | collective-permute-start | bytes 196616 | tf_op jit(solution)/shard_map/while/body/eval_jaxpr/ppermute | solution.py:11
  112.4 12.3 %collective-permute-start.1 = (f32[16,1024]{1,0:T(8,128)S(1)}, f32[16,1024]{1,0:T(8,128)}, u32[]{:S(2)}, u32[]{:S(2)}) collective-permute-start(f32[16,1024]{1,0:T(8,128)S(1)} %add.226), channel_id=1, source_target_pairs={{0,32},{32,64},{64,96},{96,128},{128,160},{160,192},{192,224},{224... | collective-permute-start | bytes 196616 | tf_op jit(solution)/shard_map/while/body/eval_jaxpr/ppermute | solution.py:11
  131.7 12.4 %collective-permute-start.1 = (f32[16,1024]{1,0:T(8,128)S(1)}, f32[16,1024]{1,0:T(8,128)}, u32[]{:S(2)}, u32[]{:S(2)}) collective-permute-start(f32[16,1024]{1,0:T(8,128)S(1)} %add.226), channel_id=1, source_target_pairs={{0,32},{32,64},{64,96},{96,128},{128,160},{160,192},{192,224},{224... | collective-permute-start | bytes 196616 | tf_op jit(solution)/shard_map/while/body/eval_jaxpr/ppermute | solution.py:11
  151.1 12.5 %collective-permute-start.1 = (f32[16,1024]{1,0:T(8,128)S(1)}, f32[16,1024]{1,0:T(8,128)}, u32[]{:S(2)}, u32[]{:S(2)}) collective-permute-start(f32[16,1024]{1,0:T(8,128)S(1)} %add.226), channel_id=1, source_target_pairs={{0,32},{32,64},{64,96},{96,128},{128,160},{160,192},{192,224},{224... | collective-permute-start | bytes 196616 | tf_op jit(solution)/shard_map/while/body/eval_jaxpr/ppermute | solution.py:11
  170.6 12.3 %collective-permute-start.1 = (f32[16,1024]{1,0:T(8,128)S(1)}, f32[16,1024]{1,0:T(8,128)}, u32[]{:S(2)}, u32[]{:S(2)}) collective-permute-start(f32[16,1024]{1,0:T(8,128)S(1)} %add.226), channel_id=1, source_target_pairs={{0,32},{32,64},{64,96},{96,128},{128,160},{160,192},{192,224},{224... | collective-permute-start | bytes 196616 | tf_op jit(solution)/shard_map/while/body/eval_jaxpr/ppermute | solution.py:11
  189.9 13.0 %collective-permute-start.1 = (f32[16,1024]{1,0:T(8,128)S(1)}, f32[16,1024]{1,0:T(8,128)}, u32[]{:S(2)}, u32[]{:S(2)}) collective-permute-start(f32[16,1024]{1,0:T(8,128)S(1)} %add.226), channel_id=1, source_target_pairs={{0,32},{32,64},{64,96},{96,128},{128,160},{160,192},{192,224},{224... | collective-permute-start | bytes 196616 | tf_op jit(solution)/shard_map/while/body/eval_jaxpr/ppermute | solution.py:11
  209.8 12.3 %collective-permute-start.1 = (f32[16,1024]{1,0:T(8,128)S(1)}, f32[16,1024]{1,0:T(8,128)}, u32[]{:S(2)}, u32[]{:S(2)}) collective-permute-start(f32[16,1024]{1,0:T(8,128)S(1)} %add.226), channel_id=1, source_target_pairs={{0,32},{32,64},{64,96},{96,128},{128,160},{160,192},{192,224},{224... | collective-permute-start | bytes 196616 | tf_op jit(solution)/shard_map/while/body/eval_jaxpr/ppermute | solution.py:11
  223.0 12.4 %collective-permute-start = (f32[16,1024]{1,0:T(8,128)S(1)}, f32[16,1024]{1,0:T(8,128)}, u32[]{:S(2)}, u32[]{:S(2)}) collective-permute-start(f32[16,1024]{1,0:T(8,128)S(1)} %copy.16), channel_id=1, source_target_pairs={{0,32},{32,64},{64,96},{96,128},{128,160},{160,192},{192,224},{224... | collective-permute-start | bytes 196616 | tf_op jit(solution)/shard_map/while/body/eval_jaxpr/ppermute | solution.py:11
  229.1 12.4 %collective-permute-start.1 = (f32[16,1024]{1,0:T(8,128)S(1)}, f32[16,1024]{1,0:T(8,128)}, u32[]{:S(2)}, u32[]{:S(2)}) collective-permute-start(f32[16,1024]{1,0:T(8,128)S(1)} %add.226), channel_id=1, source_target_pairs={{0,32},{32,64},{64,96},{96,128},{128,160},{160,192},{192,224},{224... | collective-permute-start | bytes 196616 | tf_op jit(solution)/shard_map/while/body/eval_jaxpr/ppermute | solution.py:11
  242.4 13.0 %collective-permute-start = (f32[16,1024]{1,0:T(8,128)S(1)}, f32[16,1024]{1,0:T(8,128)}, u32[]{:S(2)}, u32[]{:S(2)}) collective-permute-start(f32[16,1024]{1,0:T(8,128)S(1)} %copy.16), channel_id=1, source_target_pairs={{0,32},{32,64},{64,96},{96,128},{128,160},{160,192},{192,224},{224... | collective-permute-start | bytes 196616 | tf_op jit(solution)/shard_map/while/body/eval_jaxpr/ppermute | solution.py:11
  248.5 13.0 %collective-permute-start.1 = (f32[16,1024]{1,0:T(8,128)S(1)}, f32[16,1024]{1,0:T(8,128)}, u32[]{:S(2)}, u32[]{:S(2)}) collective-permute-start(f32[16,1024]{1,0:T(8,128)S(1)} %add.226), channel_id=1, source_target_pairs={{0,32},{32,64},{64,96},{96,128},{128,160},{160,192},{192,224},{224... | collective-permute-start | bytes 196616 | tf_op jit(solution)/shard_map/while/body/eval_jaxpr/ppermute | solution.py:11
  268.5 12.3 %collective-permute-start.1 = (f32[16,1024]{1,0:T(8,128)S(1)}, f32[16,1024]{1,0:T(8,128)}, u32[]{:S(2)}, u32[]{:S(2)}) collective-permute-start(f32[16,1024]{1,0:T(8,128)S(1)} %add.226), channel_id=1, source_target_pairs={{0,32},{32,64},{64,96},{96,128},{128,160},{160,192},{192,224},{224... | collective-permute-start | bytes 196616 | tf_op jit(solution)/shard_map/while/body/eval_jaxpr/ppermute | solution.py:11
  281.7 12.8 %collective-permute-start = (f32[16,1024]{1,0:T(8,128)S(1)}, f32[16,1024]{1,0:T(8,128)}, u32[]{:S(2)}, u32[]{:S(2)}) collective-permute-start(f32[16,1024]{1,0:T(8,128)S(1)} %copy.16), channel_id=1, source_target_pairs={{0,32},{32,64},{64,96},{96,128},{128,160},{160,192},{192,224},{224... | collective-permute-start | bytes 196616 | tf_op jit(solution)/shard_map/while/body/eval_jaxpr/ppermute | solution.py:11
  287.8 12.8 %collective-permute-start.1 = (f32[16,1024]{1,0:T(8,128)S(1)}, f32[16,1024]{1,0:T(8,128)}, u32[]{:S(2)}, u32[]{:S(2)}) collective-permute-start(f32[16,1024]{1,0:T(8,128)S(1)} %add.226), channel_id=1, source_target_pairs={{0,32},{32,64},{64,96},{96,128},{128,160},{160,192},{192,224},{224... | collective-permute-start | bytes 196616 | tf_op jit(solution)/shard_map/while/body/eval_jaxpr/ppermute | solution.py:11
  307.5 12.3 %collective-permute-start.1 = (f32[16,1024]{1,0:T(8,128)S(1)}, f32[16,1024]{1,0:T(8,128)}, u32[]{:S(2)}, u32[]{:S(2)}) collective-permute-start(f32[16,1024]{1,0:T(8,128)S(1)} %add.226), channel_id=1, source_target_pairs={{0,32},{32,64},{64,96},{96,128},{128,160},{160,192},{192,224},{224... | collective-permute-start | bytes 196616 | tf_op jit(solution)/shard_map/while/body/eval_jaxpr/ppermute | solution.py:11
  326.8 12.4 %collective-permute-start.1 = (f32[16,1024]{1,0:T(8,128)S(1)}, f32[16,1024]{1,0:T(8,128)}, u32[]{:S(2)}, u32[]{:S(2)}) collective-permute-start(f32[16,1024]{1,0:T(8,128)S(1)} %add.226), channel_id=1, source_target_pairs={{0,32},{32,64},{64,96},{96,128},{128,160},{160,192},{192,224},{224... | collective-permute-start | bytes 196616 | tf_op jit(solution)/shard_map/while/body/eval_jaxpr/ppermute | solution.py:11
  (46 other events, 561.6 us)
Sparse Core Ops, SparseCore 0:
  339.3 54.8 all-gather.2
